TPU v7x, 32 devices: a whole 2x2x4 slice. The times are simulated.
32 devices in a mesh: groups: 2 (over y), tm: 4 (over z), heads: 4 (over x, core).
Axes of the slice: x: 2, y: 2, z: 4, core: 2. Of those that a mesh axis runs over, the one named last changes fastest.
Arguments:
- wave_feats: bfloat16 [5120, 512], P(('groups', 'tm')), parts along dimension 0, may hold values from -6 to 6
- conv_weight: bfloat16 [2, 512, 512], P(None, None, 'heads'), may hold values from -0.1875 to 0.1875
- proj_weight: bfloat16 [512, 1280], P('heads'), may hold values from -0.25 to 0.25
- ln_gain: float32 [1280], replicated, may hold values from 0.1 to 1.9
- qkv_weight: bfloat16 [1280, 3, 1280], P(None, None, 'heads'), may hold values from -1 to 1
- out_weight: bfloat16 [1280, 1280], P(None, 'heads'), may hold values from -0.15625 to 0.15625
- depth_weight: float32 [31, 1280], P(None, 'heads'), may hold values from -1 to 1
- depth_scale: float32 [1280], P('heads'), may hold values from 0.5 to 2
- depth_shift: float32 [1280], P('heads'), may hold values from -3 to 3
- seg_ids: int32 [2560], P('groups'), parts along dimension 0, may hold values from 0 to 7, never falling along the last dimension, each value on 1 to 320 neighbouring positions
- phrase_ids: int32 [8, 512], P('groups'), parts along dimension 0, may hold values from 0 to 8191, as said below
- counts: int32 [8], P('groups'), parts along dimension 0, may hold values from 1 to 512, 1024 in all
- phrase_store: bfloat16 [8192, 2, 1280], P('tm', None, 'heads'), may hold values from -9 to 9
Outputs:
- scored: bfloat16 [2560, 1280], P(('groups', 'tm'), 'heads'), parts along dimension 0
There are 2 independent parts, one for each index of `groups`. A program takes and returns all parts, laid end to end along the dimension named above; an argument that names none is the same for every part. Nothing has to cross between parts.
Inputs may be any that keep to these rules, and one draw needn't show every extreme that they name: `phrase_ids`: each segment's list names phrases of exactly 2 owners, exactly 256 slots for each of them, the owner of phrase p being p // 2048; ids may repeat.
All inputs are finite; a program needn't handle non-finite values.
Results may differ from a plain program's by a relative error of at most 0.0085.
The roundings to bfloat16 on the way count: a program that leaves them out, or rounds other values in their place, can miss the bound.
Values may be sent and summed in bfloat16 or wider, within the bound.
A program may use at most 64 MiB of HBM per device.

v0:
```python
import math
import jax
import jax.numpy as jnp
from jax import lax
from jax.sharding import PartitionSpec as P

HEAD_DIM = 64


def extended(cells, sides, width):
    for axis, dim in sides:
        count = lax.axis_size(axis)
        ends = count - 1
        head = lax.slice_in_dim(cells, 0, width, axis=dim)
        tail = lax.slice_in_dim(cells, cells.shape[dim] - width, cells.shape[dim], axis=dim)
        cells = jnp.concatenate(
            [
                lax.ppermute(tail, axis, [(i, (i + 1) % count) for i in range(ends)]),
                cells,
                lax.ppermute(head, axis, [((i + 1) % count, i) for i in range(ends)]),
            ],
            axis=dim,
        )
    return cells


def layer_norm(values, gain):
    centre = jnp.mean(values, axis=-1, keepdims=True)
    centred = values - centre
    variance = jnp.mean(centred * centred, axis=-1, keepdims=True)
    return centred * lax.rsqrt(variance + 1e-05) * gain


def attend(queries, keys_all, values_all, allowed):
    query_heads = queries.reshape(queries.shape[0], -1, HEAD_DIM)
    key_heads = keys_all.reshape(keys_all.shape[0], -1, HEAD_DIM)
    value_heads = values_all.reshape(values_all.shape[0], -1, HEAD_DIM)
    scores = jnp.einsum(
        "qhd,khd->hqk", query_heads, key_heads, preferred_element_type=jnp.float32
    ) / math.sqrt(HEAD_DIM)
    scores = jnp.where(allowed[None], scores, -1e30)
    highest = jnp.max(scores, axis=-1, keepdims=True)
    raised = jnp.where(allowed[None], jnp.exp(scores - highest), 0.0)
    weights = (raised / jnp.sum(raised, axis=-1, keepdims=True)).astype(jnp.bfloat16)
    output = jnp.einsum("hqk,khd->qhd", weights, value_heads, preferred_element_type=jnp.float32)
    return output.reshape(queries.shape[0], -1).astype(jnp.bfloat16)


def body(
    wave_feats,
    conv_weight,
    proj_weight,
    ln_gain,
    qkv_weight,
    out_weight,
    depth_weight,
    depth_scale,
    depth_shift,
    seg_ids,
    phrase_ids,
    counts,
    phrase_store,
):
    seg_rows = wave_feats.shape[0] // 2
    channels = wave_feats.shape[1]
    head_cols = qkv_weight.shape[2]
    frame_pairs = wave_feats.reshape(seg_rows, 2 * channels)
    conv_out = jax.nn.gelu(
        jnp.dot(
            frame_pairs, conv_weight.reshape(2 * channels, -1), preferred_element_type=jnp.float32
        ),
        approximate=False,
    ).astype(jnp.bfloat16)
    partial_sum = jnp.dot(conv_out, proj_weight, preferred_element_type=jnp.float32)
    hidden = lax.psum(partial_sum, "heads").astype(jnp.bfloat16)
    normed = layer_norm(hidden.astype(jnp.float32), ln_gain).astype(jnp.bfloat16)
    proj_qkv = jnp.einsum(
        "fd,djc->fjc", normed, qkv_weight, preferred_element_type=jnp.float32
    ).astype(jnp.bfloat16)
    window_kv = extended(proj_qkv[:, 1:3], (("tm", 0),), seg_rows)
    segment = lax.axis_index("tm")
    segments = lax.axis_size("tm")
    padded_ids = jnp.pad(seg_ids, (seg_rows, seg_rows), constant_values=-1)
    window_ids = lax.dynamic_slice_in_dim(padded_ids, segment * seg_rows, 3 * seg_rows, 0)
    own_ids = lax.dynamic_slice_in_dim(seg_ids, segment * seg_rows, seg_rows, 0)
    slots = phrase_ids.shape[1]
    capacity = 2 * slots // segments
    store_rows = phrase_store.shape[0]
    owners = phrase_ids // store_rows
    local_rows = phrase_ids % store_rows
    held_here = owners == segment
    held_rank = jnp.cumsum(held_here.astype(jnp.int32), axis=1) - 1
    target_slot = jnp.where(held_here, held_rank, capacity)
    source_row = jnp.broadcast_to(jnp.arange(segments, dtype=jnp.int32)[:, None], phrase_ids.shape)
    requests = (
        jnp.zeros((segments, capacity), jnp.int32)
        .at[source_row, target_slot]
        .set(local_rows, mode="drop")
    )
    outgoing = phrase_store[requests]
    incoming = lax.all_to_all(outgoing, "tm", split_axis=0, concat_axis=0, tiled=True)
    my_list = lax.dynamic_index_in_dim(phrase_ids, segment, 0, keepdims=False)
    my_owner = my_list // store_rows
    shared_owner = my_owner[:, None] == my_owner[None, :]
    slot_index = jnp.arange(slots, dtype=jnp.int32)
    earlier_slot = slot_index[None, :] < slot_index[:, None]
    my_rank = jnp.sum(jnp.logical_and(shared_owner, earlier_slot), axis=1)
    fetched = incoming.reshape(segments * capacity, 2, head_cols)[my_owner * capacity + my_rank]
    live_slots = slot_index < counts[segment]
    frame_mask = own_ids[:, None] == window_ids[None, :]
    allowed = jnp.concatenate(
        [frame_mask, jnp.broadcast_to(live_slots[None, :], (seg_rows, slots))], axis=1
    )
    keys_all = jnp.concatenate([window_kv[:, 0], fetched[:, 0]], axis=0)
    values_all = jnp.concatenate([window_kv[:, 1], fetched[:, 1]], axis=0)
    attended = attend(proj_qkv[:, 0], keys_all, values_all, allowed)
    branch_out = jnp.dot(
        lax.all_gather(attended, "heads", axis=1, tiled=True),
        out_weight,
        preferred_element_type=jnp.float32,
    )
    own_cols = lax.dynamic_slice_in_dim(hidden, lax.axis_index("heads") * head_cols, head_cols, 1)
    mixed = (own_cols.astype(jnp.float32) + branch_out).astype(jnp.bfloat16)
    kernel_taps = depth_weight.shape[0]
    widened = extended(mixed, (("tm", 0),), kernel_taps // 2).astype(jnp.float32)
    depth_sum = jnp.zeros((seg_rows, head_cols), jnp.float32)
    for tap_index in range(kernel_taps):
        depth_sum = depth_sum + widened[tap_index : tap_index + seg_rows] * depth_weight[tap_index]
    return (mixed.astype(jnp.float32) + jax.nn.silu(depth_sum * depth_scale + depth_shift)).astype(
        jnp.bfloat16
    )


def solution(mesh):
    in_specs = (
        P(("groups", "tm"), None),
        P(None, None, "heads"),
        P("heads", None),
        P(),
        P(None, None, "heads"),
        P(None, "heads"),
        P(None, "heads"),
        P("heads"),
        P("heads"),
        P("groups"),
        P("groups", None),
        P("groups"),
        P("tm", None, "heads"),
    )
    out_specs = P(("groups", "tm"), "heads")
    return jax.shard_map(body, mesh=mesh, in_specs=in_specs, out_specs=out_specs, check_vma=False)
```

profile of v0, /device:TPU:0, one launch (start us, length us, event | category | flops | bytes accessed | tf_op | source)
XLA Modules:
  0.0 177.8 jit_solution(10112746698608492671)
XLA Ops:
  0.0 1.5 reshape.168
  1.5 3.5 %fusion.67 = f32[320,1280]{1,0:T(8,128)} fusion(bf16[128,1280]{1,0:T(8,128)(2,1)} %param.15, bf16[320,1024]{1,0:T(8,128)(2,1)S(1)} %reshape.168, bf16[1024,128]{1,0:T(8,128)(2,1)} %bitcast.72), kind=kOutput, calls=%fused_computation.123 | convolution fusion | flops 191406080 | bytes 2883584 | tf_op jit(solution)/shard_map/dot_general | solution.py:74
  4.9 36.0 %all-reduce.2 = bf16[320,1280]{1,0:T(8,128)(2,1)S(1)} all-reduce(f32[320,1280]{1,0:T(8,128)} %fusion.67), channel_id=1, replica_groups=mesh['groups'=2,'tm'=4,'heads'=4] {'heads'}, use_global_device_ids=true, to_apply=%region_0.0 | all-reduce | flops 409600 | bytes 2457600 | tf_op jit(solution)/shard_map/psum | solution.py:75
  41.0 0.2 convert_reduce_fusion
  41.2 0.4 fusion.10
  41.6 1.6 convolution_convert_fusion
  43.2 0.9 copy-done.1
  44.1 0.9 slice.292
  45.0 1.3 collective-permute-start.1
  46.2 5.4 %collective-permute-start = (bf16[320,2,320]{0,2,1:T(8,128)(2,1)}, bf16[320,2,320]{0,2,1:T(8,128)(2,1)}, u32[]{:S(2)}, u32[]{:S(2)}) collective-permute-start(bf16[320,2,320]{0,2,1:T(8,128)(2,1)} %slice.292), channel_id=1, source_target_pairs={{0,4},{4,8},{8,12},{1,5},{5,9},{9,13},{2,6},{6,10},{10,14},{3,7},{... | collective-permute-start | bytes 1228808 | tf_op jit(solution)/shard_map/ppermute | solution.py:18
  51.7 1.2 reduce-window.6
  52.9 0.2 slice_reduce_fusion
  53.1 0.2 reduce-window.9
  53.3 0.1 add_bitcast_fusion
  53.4 0.1 and_reduce_fusion
  53.5 0.1 multiply_reduce_fusion
  53.6 8.0 %scatter_custom_fusion = s32[1024]{0:T(1024)S(1)} fusion(s32[2048]{0:T(1024)S(1)} %bitcast.71, s32[2048]{0:T(1024)S(1)} %bitcast.70, s32[]{:T(128)} %constant.132.clone.1), kind=kCustom, calls=%fused_computation.193 | custom fusion | bytes 4100
  61.7 8.7 %copy.22 = bf16[2048,2,320]{2,1,0:T(2,128)(2,1)} copy(bf16[2048,2,320]{0,2,1:T(8,128)(2,1)} %param.25) | data formatting | bytes 5242880 | tf_op args[12]
  70.4 11.6 %gather_fusion = bf16[1024,2,320]{2,1,0:T(2,128)(2,1)} fusion(bf16[2048,2,320]{2,1,0:T(2,128)(2,1)} %copy.22, s32[1024]{0:T(1024)S(1)} %broadcast_clamp_fusion), kind=kCustom, calls=%fused_computation | custom fusion | bytes 2625536 | tf_op jit(solution)/shard_map/gather | solution.py:100
  81.9 4.8 %copy.23 = bf16[4,256,2,320]{1,3,2,0:T(8,128)(2,1)} copy(bf16[4,256,2,320]{3,2,1,0:T(2,128)(2,1)} %bitcast.56) | data formatting | bytes 2621440 | tf_op jit(solution)/shard_map/gather | solution.py:100
  86.7 4.6 %all-to-all-start = ((bf16[4,256,2,320]{1,3,2,0:T(8,128)(2,1)}), bf16[4,256,2,320]{1,3,2,0:T(8,128)(2,1)}, u32[]{:S(2)}, u32[]{:S(2)}) async-start(bf16[4,256,2,320]{1,3,2,0:T(8,128)(2,1)} %copy.23), calls=%async_computation | async-start | bytes 2621440 | tf_op jit(solution)/shard_map/all_to_all | solution.py:101
  91.4 0.6 dynamic_slice.20
  92.0 0.1 pad_dynamic-slice_fusion
  92.1 0.6 iota_compare_fusion.1
  92.7 0.1 dynamic_slice.18
  92.8 0.1 pad.11.clone
  92.9 0.3 convert_reduce_fusion.1
  93.2 0.7 slice_reduce_fusion.31
  93.9 0.2 broadcast_compare_fusion
  94.1 1.0 pad_add_fusion
  95.1 1.7 pad_maximum_fusion
  96.9 1.2 fusion.147
  98.1 24.9 %all-to-all-done = bf16[4,256,2,320]{1,3,2,0:T(8,128)(2,1)} async-done(((bf16[4,256,2,320]{1,3,2,0:T(8,128)(2,1)}), bf16[4,256,2,320]{1,3,2,0:T(8,128)(2,1)}, u32[]{:S(2)}, u32[]{:S(2)}) %all-to-all-start) | async-done | bytes 1310752 | tf_op jit(solution)/shard_map/all_to_all | solution.py:101
  122.9 4.9 %copy.24 = bf16[4,256,2,320]{3,2,1,0:T(2,128)(2,1)} copy(bf16[4,256,2,320]{1,3,2,0:T(8,128)(2,1)} %all-to-all-done) | data formatting | bytes 2621440 | tf_op jit(solution)/shard_map/all_to_all | solution.py:101
  127.8 4.7 %gather_fusion.1 = bf16[512,2,320]{2,1,0:T(2,128)(2,1)} fusion(bf16[1024,2,320]{2,1,0:T(2,128)(2,1)} %bitcast.57, s32[1024]{0:T(1024)S(1)} %pad_clamp_fusion), kind=kCustom, calls=%fused_computation.1 | custom fusion | bytes 1312768 | tf_op jit(solution)/shard_map/gather | solution.py:108
  132.5 3.9 %fusion.148 = (bf16[512,1,320]{2,1,0:T(2,128)(2,1)}, bf16[512,1,320]{2,1,0:T(2,128)(2,1)}) fusion(bf16[512,2,320]{2,1,0:T(2,128)(2,1)} %gather_fusion.1), kind=kLoop, calls=%fused_computation.269 | loop fusion | bytes 1310720 | tf_op jit(solution)/shard_map/slice | solution.py:115
  136.5 2.8 %copy.25 = bf16[512,1,320]{0,2,1:T(8,128)(2,1)} copy(bf16[512,1,320]{2,1,0:T(2,128)(2,1)} %get-tuple-element.42) | data formatting | bytes 655360 | tf_op jit(solution)/shard_map/slice | solution.py:115
  139.3 2.8 %copy.26 = bf16[512,1,320]{0,2,1:T(8,128)(2,1)} copy(bf16[512,1,320]{2,1,0:T(2,128)(2,1)} %get-tuple-element.43) | data formatting | bytes 655360 | tf_op jit(solution)/shard_map/slice | solution.py:114
  142.1 10.1 %fusion.150 = (f32[5,320]{1,0:T(8,128)}, f32[5,320,1472]{2,1,0:T(8,128)}) fusion(pred[320,1472]{1,0:T(8,128)(4,1)} %pad_add_fusion, bf16[320,5,64]{0,2,1:T(8,128)(2,1)S(1)} %bitcast.58, bf16[512,5,64]{0,2,1:T(8,128)(2,1)} %bitcast.62, bf16[960,5,64]{0,2,1:T(8,128)(2,1)} %bitcast.60), kind=kOutput, calls=%fused_computation.271 | convolution fusion | flops 315127232 | bytes 11045120 | tf_op jit(solution)/shard_map/sub | solution.py:43
  152.2 5.7 %fusion.14 = bf16[5,64,320]{2,1,0:T(8,128)(2,1)S(1)} fusion(f32[5,320,1472]{2,1,0:T(8,128)} %get-tuple-element.47, f32[5,320]{1,0:T(8,128)} %get-tuple-element.46, bf16[512,5,64]{0,2,1:T(8,128)(2,1)} %bitcast.61, bf16[960,5,64]{0,2,1:T(8,128)(2,1)} %bitcast.59), kind=kOutput, calls=%fused_computation.25 | convolution fusion | flops 308162560 | bytes 10574080 | tf_op jit(solution)/shard_map/hqk,khd->qhd/dot_general | solution.py:45
  157.9 9.1 %all_gather.3 = bf16[320,1280]{0,1:T(8,128)(2,1)S(1)} all-gather(bf16[320,320]{0,1:T(8,128)(2,1)S(1)} %bitcast.63), channel_id=1, replica_groups=mesh['groups'=2,'tm'=4,'heads'=4] {'heads'}, dimensions={1}, use_global_device_ids=true | all-gather | bytes 1024000 | tf_op jit(solution)/shard_map/all_gather | solution.py:118
  167.2 0.7 fusion.13
  167.9 1.3 collective-permute-start.2
  169.2 1.3 collective-permute-start.3
  170.5 1.0 slice_reduce_fusion.30
  171.6 3.2 %collective-permute-done.3 = bf16[15,320]{1,0:T(8,128)(2,1)S(1)} collective-permute-done((bf16[15,320]{1,0:T(8,128)(2,1)S(1)}, bf16[15,320]{1,0:T(8,128)(2,1)S(1)}, u32[]{:S(2)}, u32[]{:S(2)}) %collective-permute-start.3) | collective-permute-done | bytes 9632 | tf_op jit(solution)/shard_map/ppermute | solution.py:20
  174.8 0.1 maximum_convert_fusion
  175.0 2.8 %add_convert_fusion = bf16[320,320]{1,0:T(8,128)(2,1)} fusion(bf16[320,320]{1,0:T(8,128)(2,1)S(1)} %fusion.13, f32[350,320]{1,0:T(8,128)S(1)} %maximum_convert_fusion, f32[320]{0:T(512)S(1)} %copy-done.16, f32[320]{0:T(512)S(1)} %copy-done.17, f32[320]{0:T(512)S(1)} %get-tuple-element.34, f32[320]{0:T(512)S(1)} %get-tuple-element.35, ...), kind=kLoop, calls=%fused_computation.102 | loop fusion | flops 7168000 | bytes 13149440 | tf_op jit(solution)/shard_map/convert_element_type | solution.py:129
  (69 shorter events, 0.3 us)
Async XLA Ops:
  0.0 41.6 %copy-start = (bf16[1280,3,320]{0,2,1:T(8,128)(2,1)S(1)}, bf16[1280,3,320]{0,2,1:T(8,128)(2,1)}, u32[]{:S(2)}) copy-start(bf16[1280,3,320]{0,2,1:T(8,128)(2,1)} %param.17) | copy-start | bytes 7372804
  4.9 36.7 %copy-start.21 = (f32[1280]{0:T(1024)S(1)}, f32[1280]{0:T(1024)}, u32[]{:S(2)}) copy-start(f32[1280]{0:T(1024)} %param.16) | copy-start | bytes 15364
  41.6 10.0 %copy-start.3 = (s32[4,512]{1,0:T(4,128)S(1)}, s32[4,512]{1,0:T(4,128)}, u32[]{:S(2)}) copy-start(s32[4,512]{1,0:T(4,128)} %param.23) | copy-start | bytes 24580
  41.6 11.8 %copy-start.19 = (s32[2]{0:T(128)S(1)}, s32[2]{0:T(128)}, u32[]{:S(2)}) copy-start(s32[2]{0:T(128)} %constant.156) | copy-start | bytes 28
  41.6 11.9 %copy-start.18 = (s32[2]{0:T(128)S(1)}, s32[2]{0:T(128)}, u32[]{:S(2)}) copy-start(s32[2]{0:T(128)} %constant.153) | copy-start | bytes 28
  43.2 0.9 copy-start.1
  45.0 50.2 %collective-permute-start.1 = (bf16[320,2,320]{0,2,1:T(8,128)(2,1)}, bf16[320,2,320]{0,2,1:T(8,128)(2,1)}, u32[]{:S(2)}, u32[]{:S(2)}) collective-permute-start(bf16[320,2,320]{0,2,1:T(8,128)(2,1)} %slice.292), channel_id=1, source_target_pairs={{4,0},{8,4},{12,8},{5,1},{9,5},{13,9},{6,2},{10,6},{14,10},{7,3},{... | collective-permute-start | bytes 1228808 | tf_op jit(solution)/shard_map/ppermute | solution.py:20
  46.2 48.9 %collective-permute-start = (bf16[320,2,320]{0,2,1:T(8,128)(2,1)}, bf16[320,2,320]{0,2,1:T(8,128)(2,1)}, u32[]{:S(2)}, u32[]{:S(2)}) collective-permute-start(bf16[320,2,320]{0,2,1:T(8,128)(2,1)} %slice.292), channel_id=1, source_target_pairs={{0,4},{4,8},{8,12},{1,5},{5,9},{9,13},{2,6},{6,10},{10,14},{3,7},{... | collective-permute-start | bytes 1228808 | tf_op jit(solution)/shard_map/ppermute | solution.py:18
  86.7 4.7 %copy-start.22 = (s32[4]{0:T(128)S(1)}, s32[4]{0:T(128)}, u32[]{:S(2)}) copy-start(s32[4]{0:T(128)} %param.24) | copy-start | bytes 52
  86.7 5.3 %copy-start.4 = (s32[1280]{0:T(1024)S(1)}, s32[1280]{0:T(1024)}, u32[]{:S(2)}) copy-start(s32[1280]{0:T(1024)} %param.22) | copy-start | bytes 15364
  86.7 6.5 %copy-start.2 = (f32[31,320]{1,0:T(8,128)S(1)}, f32[31,320]{1,0:T(8,128)}, u32[]{:S(2)}) copy-start(f32[31,320]{1,0:T(8,128)} %param.19) | copy-start | bytes 119044
  86.7 36.2 %all-to-all-start = ((bf16[4,256,2,320]{1,3,2,0:T(8,128)(2,1)}), bf16[4,256,2,320]{1,3,2,0:T(8,128)(2,1)}, u32[]{:S(2)}, u32[]{:S(2)}) async-start(bf16[4,256,2,320]{1,3,2,0:T(8,128)(2,1)} %copy.23), calls=%async_computation | async-start | bytes 2621440 | tf_op jit(solution)/shard_map/all_to_all | solution.py:101
  132.5 9.6 %slice-start = ((bf16[320,3,320]{0,2,1:T(8,128)(2,1)}), bf16[320,1,320]{0,2,1:T(8,128)(2,1)S(1)}, s32[]{:S(2)}) async-start(bf16[320,3,320]{0,2,1:T(8,128)(2,1)} %copy-done.1), calls=%async_computation.1 | async-start | bytes 491520 | tf_op jit(solution)/shard_map/slice | solution.py:116
  152.2 14.8 %copy-start.20 = (bf16[1280,320]{0,1:T(8,128)(2,1)S(1)}, bf16[1280,320]{0,1:T(8,128)(2,1)}, u32[]{:S(2)}) copy-start(bf16[1280,320]{0,1:T(8,128)(2,1)} %param.18) | copy-start | bytes 2457604
  167.0 7.8 %copy-start.5 = (f32[320]{0:T(512)S(1)}, f32[320]{0:T(512)}, u32[]{:S(2)}) copy-start(f32[320]{0:T(512)} %get-tuple-element.13) | copy-start | bytes 3844
  167.0 7.8 %copy-start.6 = (f32[320]{0:T(512)S(1)}, f32[320]{0:T(512)}, u32[]{:S(2)}) copy-start(f32[320]{0:T(512)} %get-tuple-element.14) | copy-start | bytes 3844
  167.0 7.8 %copy-start.7 = (f32[320]{0:T(512)S(1)}, f32[320]{0:T(512)}, u32[]{:S(2)}) copy-start(f32[320]{0:T(512)} %get-tuple-element.15) | copy-start | bytes 3844
  167.0 7.8 %copy-start.8 = (f32[320]{0:T(512)S(1)}, f32[320]{0:T(512)}, u32[]{:S(2)}) copy-start(f32[320]{0:T(512)} %get-tuple-element.16) | copy-start | bytes 3844
  167.1 7.8 %copy-start.9 = (f32[320]{0:T(512)S(1)}, f32[320]{0:T(512)}, u32[]{:S(2)}) copy-start(f32[320]{0:T(512)} %get-tuple-element.17) | copy-start | bytes 3844
  167.1 7.8 %copy-start.10 = (f32[320]{0:T(512)S(1)}, f32[320]{0:T(512)}, u32[]{:S(2)}) copy-start(f32[320]{0:T(512)} %get-tuple-element.18) | copy-start | bytes 3844
  167.1 7.8 %copy-start.11 = (f32[320]{0:T(512)S(1)}, f32[320]{0:T(512)}, u32[]{:S(2)}) copy-start(f32[320]{0:T(512)} %get-tuple-element.19) | copy-start | bytes 3844
  167.1 7.8 %copy-start.12 = (f32[320]{0:T(512)S(1)}, f32[320]{0:T(512)}, u32[]{:S(2)}) copy-start(f32[320]{0:T(512)} %get-tuple-element.20) | copy-start | bytes 3844
  167.1 7.8 %copy-start.13 = (f32[320]{0:T(512)S(1)}, f32[320]{0:T(512)}, u32[]{:S(2)}) copy-start(f32[320]{0:T(512)} %get-tuple-element.21) | copy-start | bytes 3844
  167.1 7.8 %copy-start.14 = (f32[320]{0:T(512)S(1)}, f32[320]{0:T(512)}, u32[]{:S(2)}) copy-start(f32[320]{0:T(512)} %get-tuple-element.22) | copy-start | bytes 3844
  167.1 7.8 %copy-start.15 = (f32[320]{0:T(512)S(1)}, f32[320]{0:T(512)}, u32[]{:S(2)}) copy-start(f32[320]{0:T(512)} %get-tuple-element.23) | copy-start | bytes 3844
  167.1 7.8 %copy-start.16 = (f32[320]{0:T(512)S(1)}, f32[320]{0:T(512)}, u32[]{:S(2)}) copy-start(f32[320]{0:T(512)} %param.21) | copy-start | bytes 3844
  167.1 7.8 %copy-start.17 = (f32[320]{0:T(512)S(1)}, f32[320]{0:T(512)}, u32[]{:S(2)}) copy-start(f32[320]{0:T(512)} %param.20) | copy-start | bytes 3844
  167.9 3.7 %collective-permute-start.2 = (bf16[15,320]{1,0:T(8,128)(2,1)S(1)}, bf16[15,320]{1,0:T(8,128)(2,1)S(1)}, u32[]{:S(2)}, u32[]{:S(2)}) collective-permute-start(bf16[15,320]{1,0:T(8,128)(2,1)S(1)} %get-tuple-element.44), channel_id=1, source_target_pairs={{0,4},{4,8},{8,12},{1,5},{5,9},{9,13},{2,6},{6,10},{10,14},{3,7},{... | collective-permute-start | bytes 28808 | tf_op jit(solution)/shard_map/ppermute | solution.py:18
  169.2 5.6 %collective-permute-start.3 = (bf16[15,320]{1,0:T(8,128)(2,1)S(1)}, bf16[15,320]{1,0:T(8,128)(2,1)S(1)}, u32[]{:S(2)}, u32[]{:S(2)}) collective-permute-start(bf16[15,320]{1,0:T(8,128)(2,1)S(1)} %get-tuple-element.45), channel_id=1, source_target_pairs={{4,0},{8,4},{12,8},{5,1},{9,5},{13,9},{6,2},{10,6},{14,10},{7,3},{... | collective-permute-start | bytes 28808 | tf_op jit(solution)/shard_map/ppermute | solution.py:20
where the time goes:
time: 179 us; the launch traced here: 178 us
  local copies, waits for them, and re-layouts  59.6 us (33%)
  blocking collectives  45.1 us (25%)
  waiting for transfers between devices  28.1 us (16%)
  matrix products  21.5 us (12%)
  starting transfers between devices  13.8 us (8%)
  other arithmetic  9.11 us (5%)
    psum x1, blocking collectives, body(): hidden = lax.psum(partial_sum, 'heads').astype(jnp.bfloat16)  36 us
    all_to_all x1, waiting for transfers between devices, body(): lax.all_to_all(outgoing, 'tm', split_axis=0, concat_axis=0, tiled=True)  24.9 us
    unnamed x51, local copies, waits for them, and re-layouts  17.7 us
    gather x2, local copies, waits for them, and re-layouts, body(): outgoing = phrase_store[requests]  16.4 us
    sub x1, matrix products, attend(): raised = jnp.where(allowed[None], jnp.exp(scores - highest), 0.0)  10.1 us
    all_gather x1, blocking collectives, body(): lax.all_gather(attended, 'heads', axis=1, tiled=True)  9.1 us
    slice x3, local copies, waits for them, and re-layouts, body(): values_all = jnp.concatenate([window_kv[:, 1], fetched[:, 1]], axis=0)  7.92 us
    ppermute x2, starting transfers between devices, extended(): lax.ppermute(tail, axis, [(i, (i + 1) % count) for i in range(ends)])  6.66 us
  transfers between devices with their start and end apart: 5, of which 2 were waited for; matrix products, arithmetic and copies ran while one was open for 24% of the time, Pallas kernels for 0%

commit v1 on v0

--- a/solution.py
+++ b/solution.py
@@ -72,7 +72,7 @@
         approximate=False,
     ).astype(jnp.bfloat16)
     partial_sum = jnp.dot(conv_out, proj_weight, preferred_element_type=jnp.float32)
-    hidden = lax.psum(partial_sum, "heads").astype(jnp.bfloat16)
+    hidden = jnp.sum(lax.all_gather(partial_sum, "heads"), axis=0).astype(jnp.bfloat16)
     normed = layer_norm(hidden.astype(jnp.float32), ln_gain).astype(jnp.bfloat16)
     proj_qkv = jnp.einsum(
         "fd,djc->fjc", normed, qkv_weight, preferred_element_type=jnp.float32

time: 179 us -> 152 us (0.85)
  blocking collectives: 45.1 us -> 9.64 us
  between operations: 0.5 us -> 13.9 us
  waiting for transfers between devices: 28.1 us -> 18.1 us
  other arithmetic: 9.11 us -> 12.5 us
    psum x1 -> x0, blocking collectives: 36 us -> none  [body(): hidden = lax.psum(partial_sum, 'heads').astype(jnp.bfloat16)]
    all_to_all x1, waiting for transfers between devices: 24.9 us -> 9.62 us  [body(): lax.all_to_all(outgoing, 'tm', split_axis=0, concat_axis=0, tiled=True)]
    all_gather x0 -> x1, waiting for transfers between devices: none -> 5.2 us  [body(): lax.all_gather(partial_sum, 'heads')]
    reduce_sum x0 -> x1, other arithmetic: none -> 3.37 us  [body(): jnp.sum(lax.all_gather(partial_sum, 'heads'), axis=0).astype(jnp.bfloat16)]
  transfers between devices with their start and end apart: 5 -> 6, of which waited for: 2 -> 3; matrix products, arithmetic and copies ran while one was open for 24% -> 43% of each run, Pallas kernels for 0% -> 0%
where the time goes in v1:
time: 152 us; the launch traced here: 151 us
  local copies, waits for them, and re-layouts  59.8 us (39%)
  matrix products  21.5 us (14%)
  waiting for transfers between devices  18.1 us (12%)
  starting transfers between devices  15.5 us (10%)
  between operations  13.9 us (9%)
  other arithmetic  12.5 us (8%)
  blocking collectives  9.64 us (6%)
    unnamed x51, local copies, waits for them, and re-layouts  17.9 us
    gather x2, local copies, waits for them, and re-layouts, body(): outgoing = phrase_store[requests]  16.4 us
    sub x1, matrix products, attend(): raised = jnp.where(allowed[None], jnp.exp(scores - highest), 0.0)  10.1 us
    all_gather x1, blocking collectives, body(): lax.all_gather(attended, 'heads', axis=1, tiled=True)  9.64 us
    all_to_all x1, waiting for transfers between devices, body(): lax.all_to_all(outgoing, 'tm', split_axis=0, concat_axis=0, tiled=True)  9.62 us
    slice x3, local copies, waits for them, and re-layouts, body(): values_all = jnp.concatenate([window_kv[:, 1], fetched[:, 1]], axis=0)  7.9 us
    ppermute x2, starting transfers between devices, extended(): lax.ppermute(tail, axis, [(i, (i + 1) % count) for i in range(ends)])  6.62 us
    all_to_all x1, starting transfers between devices, body(): lax.all_to_all(outgoing, 'tm', split_axis=0, concat_axis=0, tiled=True)  6.35 us
  transfers between devices with their start and end apart: 6, of which 3 were waited for; matrix products, arithmetic and copies ran while one was open for 43% of the time, Pallas kernels for 0%

profile of v1, /device:TPU:0, one launch (start us, length us, event | category | flops | bytes accessed | tf_op | source)
XLA Modules:
  0.0 150.9 jit_solution(17919576872239648931)
XLA Ops:
  6.5 1.5 reshape.168
  8.0 3.4 %fusion.67 = f32[320,1280]{1,0:T(8,128)} fusion(bf16[128,1280]{1,0:T(8,128)(2,1)} %param.15, bf16[320,1024]{1,0:T(8,128)(2,1)S(1)} %reshape.168, bf16[1024,128]{1,0:T(8,128)(2,1)} %bitcast.74), kind=kOutput, calls=%fused_computation.123 | convolution fusion | flops 191406080 | bytes 2883584 | tf_op jit(solution)/shard_map/dot_general | solution.py:74
  11.6 1.2 reduce-window.6
  12.8 0.2 slice_reduce_fusion
  13.0 0.2 reduce-window.9
  13.2 0.1 add_bitcast_fusion
  13.3 0.1 multiply_reduce_fusion
  13.4 0.1 and_reduce_fusion
  13.5 8.0 %scatter_custom_fusion = s32[1024]{0:T(1024)S(1)} fusion(s32[2048]{0:T(1024)S(1)} %bitcast.73, s32[2048]{0:T(1024)S(1)} %bitcast.72, s32[]{:T(128)} %constant.132.clone.1), kind=kCustom, calls=%fused_computation.193 | custom fusion | bytes 4100
  21.6 8.9 %copy.22 = bf16[2048,2,320]{2,1,0:T(2,128)(2,1)} copy(bf16[2048,2,320]{0,2,1:T(8,128)(2,1)} %param.25) | data formatting | bytes 5242880 | tf_op args[12]
  30.5 11.6 %gather_fusion = bf16[1024,2,320]{2,1,0:T(2,128)(2,1)} fusion(bf16[2048,2,320]{2,1,0:T(2,128)(2,1)} %copy.22, s32[1024]{0:T(1024)S(1)} %broadcast_clamp_fusion), kind=kCustom, calls=%fused_computation | custom fusion | bytes 2625536 | tf_op jit(solution)/shard_map/gather | solution.py:100
  42.1 4.8 %copy.23 = bf16[4,256,2,320]{1,3,2,0:T(8,128)(2,1)} copy(bf16[4,256,2,320]{3,2,1,0:T(2,128)(2,1)} %bitcast.58) | data formatting | bytes 2621440 | tf_op jit(solution)/shard_map/gather | solution.py:100
  46.9 6.3 %all-to-all-start = ((bf16[4,256,2,320]{1,3,2,0:T(8,128)(2,1)}), bf16[4,256,2,320]{1,3,2,0:T(8,128)(2,1)}, u32[]{:S(2)}, u32[]{:S(2)}) async-start(bf16[4,256,2,320]{1,3,2,0:T(8,128)(2,1)} %copy.23), calls=%async_computation | async-start | bytes 2621440 | tf_op jit(solution)/shard_map/all_to_all | solution.py:101
  53.3 0.6 dynamic_slice.20
  53.9 0.1 pad_dynamic-slice_fusion
  54.0 0.7 slice_reduce_fusion.31
  54.7 0.3 convert_reduce_fusion.1
  54.9 0.7 iota_compare_fusion.1
  55.6 0.1 dynamic_slice.18
  55.7 0.1 pad.11.clone
  55.8 0.3 broadcast_compare_fusion
  56.0 1.0 pad_add_fusion
  57.0 5.2 %all-gather.3.cloned.1.call-done = f32[1280,1280]{1,0:T(8,128)} async-done(((f32[320,1280]{1,0:T(8,128)}), f32[1280,1280]{1,0:T(8,128)}) %all-gather.3.cloned.1.call-update) | async-done | bytes 6553616 | tf_op jit(solution)/shard_map/all_gather | solution.py:75
  62.2 3.4 %reduce_sum.47 = bf16[320,1280]{1,0:T(8,128)(2,1)S(1)} reduce(f32[4,320,1280]{2,1,0:T(8,128)} %bitcast.57, f32[]{:T(128)} %constant.59.clone.1), dimensions={0}, to_apply=%region_0.0 | reduce | flops 1228800 | bytes 7372804 | tf_op jit(solution)/shard_map/reduce_sum | solution.py:75
  65.6 0.2 convert_reduce_fusion
  65.8 0.4 fusion.10
  66.2 1.6 %convolution_convert_fusion = bf16[320,3,320]{0,2,1:T(8,128)(2,1)S(1)} fusion(bf16[1280,3,320]{0,2,1:T(8,128)(2,1)S(1)} %copy-done, bf16[320,1280]{1,0:T(8,128)(2,1)S(1)} %reduce_sum.47, f32[1280]{0:T(1024)S(1)} %copy-done.21, f32[320]{0:T(512)S(1)} %add_rsqrt_fusion, f32[320]{0:T(512)S(1)} %broadcast_multiply_fusion), kind=kOutput, calls=%fused_computation.21 | convolution fusion | flops 788787200 | bytes 3898880 | tf_op jit(solution)/shard_map/fd,djc->fjc/dot_general | solution.py:77
  67.8 0.9 copy-done.1
  68.7 0.9 slice.292
  69.5 1.3 collective-permute-start.1
  70.8 5.3 %collective-permute-start = (bf16[320,2,320]{0,2,1:T(8,128)(2,1)}, bf16[320,2,320]{0,2,1:T(8,128)(2,1)}, u32[]{:S(2)}, u32[]{:S(2)}) collective-permute-start(bf16[320,2,320]{0,2,1:T(8,128)(2,1)} %slice.292), channel_id=1, source_target_pairs={{0,4},{4,8},{8,12},{1,5},{5,9},{9,13},{2,6},{6,10},{10,14},{3,7},{... | collective-permute-start | bytes 1228808 | tf_op jit(solution)/shard_map/ppermute | solution.py:18
  76.2 9.6 %all-to-all-done = bf16[4,256,2,320]{1,3,2,0:T(8,128)(2,1)} async-done(((bf16[4,256,2,320]{1,3,2,0:T(8,128)(2,1)}), bf16[4,256,2,320]{1,3,2,0:T(8,128)(2,1)}, u32[]{:S(2)}, u32[]{:S(2)}) %all-to-all-start) | async-done | bytes 1310752 | tf_op jit(solution)/shard_map/all_to_all | solution.py:101
  85.8 4.9 %copy.24 = bf16[4,256,2,320]{3,2,1,0:T(2,128)(2,1)} copy(bf16[4,256,2,320]{1,3,2,0:T(8,128)(2,1)} %all-to-all-done) | data formatting | bytes 2621440 | tf_op jit(solution)/shard_map/all_to_all | solution.py:101
  90.7 4.7 %gather_fusion.1 = bf16[512,2,320]{2,1,0:T(2,128)(2,1)} fusion(bf16[1024,2,320]{2,1,0:T(2,128)(2,1)} %bitcast.59, s32[1024]{0:T(1024)S(1)} %pad_clamp_fusion), kind=kCustom, calls=%fused_computation.1 | custom fusion | bytes 1312768 | tf_op jit(solution)/shard_map/gather | solution.py:108
  95.4 3.9 %fusion.148 = (bf16[512,1,320]{2,1,0:T(2,128)(2,1)}, bf16[512,1,320]{2,1,0:T(2,128)(2,1)}) fusion(bf16[512,2,320]{2,1,0:T(2,128)(2,1)} %gather_fusion.1), kind=kLoop, calls=%fused_computation.269 | loop fusion | bytes 1310720 | tf_op jit(solution)/shard_map/slice | solution.py:115
  99.3 2.8 %copy.25 = bf16[512,1,320]{0,2,1:T(8,128)(2,1)} copy(bf16[512,1,320]{2,1,0:T(2,128)(2,1)} %get-tuple-element.42) | data formatting | bytes 655360 | tf_op jit(solution)/shard_map/slice | solution.py:115
  102.1 2.8 %copy.26 = bf16[512,1,320]{0,2,1:T(8,128)(2,1)} copy(bf16[512,1,320]{2,1,0:T(2,128)(2,1)} %get-tuple-element.43) | data formatting | bytes 655360 | tf_op jit(solution)/shard_map/slice | solution.py:114
  105.0 1.7 %pad_maximum_fusion = bf16[960,2,320]{0,2,1:T(8,128)(2,1)S(1)} fusion(bf16[320,2,320]{0,2,1:T(8,128)(2,1)} %collective-permute-done.1, bf16[320,2,320]{0,2,1:T(8,128)(2,1)} %slice.292, bf16[320,2,320]{0,2,1:T(8,128)(2,1)} %collective-permute-done), kind=kLoop, calls=%fused_computation.22 | loop fusion | flops 3686400 | bytes 2457600 | tf_op jit(solution)/shard_map/concatenate | solution.py:16
  106.7 1.2 fusion.147
  107.9 10.1 %fusion.150 = (f32[5,320]{1,0:T(8,128)}, f32[5,320,1472]{2,1,0:T(8,128)}) fusion(pred[320,1472]{1,0:T(8,128)(4,1)} %pad_add_fusion, bf16[320,5,64]{0,2,1:T(8,128)(2,1)S(1)} %bitcast.60, bf16[512,5,64]{0,2,1:T(8,128)(2,1)} %bitcast.64, bf16[960,5,64]{0,2,1:T(8,128)(2,1)} %bitcast.62), kind=kOutput, calls=%fused_computation.271 | convolution fusion | flops 315127232 | bytes 11045120 | tf_op jit(solution)/shard_map/sub | solution.py:43
  118.0 5.7 %fusion.14 = bf16[5,64,320]{2,1,0:T(8,128)(2,1)S(1)} fusion(f32[5,320,1472]{2,1,0:T(8,128)} %get-tuple-element.47, f32[5,320]{1,0:T(8,128)} %get-tuple-element.46, bf16[512,5,64]{0,2,1:T(8,128)(2,1)} %bitcast.63, bf16[960,5,64]{0,2,1:T(8,128)(2,1)} %bitcast.61), kind=kOutput, calls=%fused_computation.25 | convolution fusion | flops 308162560 | bytes 10574080 | tf_op jit(solution)/shard_map/hqk,khd->qhd/dot_general | solution.py:45
  123.7 9.6 %all_gather.11 = bf16[320,1280]{0,1:T(8,128)(2,1)S(1)} all-gather(bf16[320,320]{0,1:T(8,128)(2,1)S(1)} %bitcast.65), channel_id=1, replica_groups=mesh['groups'=2,'tm'=4,'heads'=4] {'heads'}, dimensions={1}, use_global_device_ids=true | all-gather | bytes 1024000 | tf_op jit(solution)/shard_map/all_gather | solution.py:118
  133.4 0.7 fusion.13
  134.2 1.3 collective-permute-start.2
  135.5 1.3 collective-permute-start.3
  136.8 1.0 slice_reduce_fusion.30
  137.8 3.2 %collective-permute-done.3 = bf16[15,320]{1,0:T(8,128)(2,1)S(1)} collective-permute-done((bf16[15,320]{1,0:T(8,128)(2,1)S(1)}, bf16[15,320]{1,0:T(8,128)(2,1)S(1)}, u32[]{:S(2)}, u32[]{:S(2)}) %collective-permute-start.3) | collective-permute-done | bytes 9632 | tf_op jit(solution)/shard_map/ppermute | solution.py:20
  141.3 2.8 %add_convert_fusion = bf16[320,320]{1,0:T(8,128)(2,1)} fusion(bf16[320,320]{1,0:T(8,128)(2,1)S(1)} %fusion.13, f32[350,320]{1,0:T(8,128)S(1)} %maximum_convert_fusion, f32[320]{0:T(512)S(1)} %copy-done.16, f32[320]{0:T(512)S(1)} %copy-done.17, f32[320]{0:T(512)S(1)} %get-tuple-element.34, f32[320]{0:T(512)S(1)} %get-tuple-element.35, ...), kind=kLoop, calls=%fused_computation.102 | loop fusion | flops 7168000 | bytes 13149440 | tf_op jit(solution)/shard_map/convert_element_type | solution.py:129
  (72 shorter events, 0.4 us)
Async XLA Ops:
  6.5 59.7 %copy-start = (bf16[1280,3,320]{0,2,1:T(8,128)(2,1)S(1)}, bf16[1280,3,320]{0,2,1:T(8,128)(2,1)}, u32[]{:S(2)}) copy-start(bf16[1280,3,320]{0,2,1:T(8,128)(2,1)} %param.17) | copy-start | bytes 7372804
  6.5 55.7 %all-gather.3.cloned.1.call-start = ((), (), s32[]{:S(2)}) async-start(), calls=%async_computation.1 | async-start | bytes 8192000 | tf_op jit(solution)/shard_map/all_gather | solution.py:75
  8.0 3.5 %copy-start.3 = (s32[4,512]{1,0:T(4,128)S(1)}, s32[4,512]{1,0:T(4,128)}, u32[]{:S(2)}) copy-start(s32[4,512]{1,0:T(4,128)} %param.23) | copy-start | bytes 24580
  8.0 5.3 %copy-start.19 = (s32[2]{0:T(128)S(1)}, s32[2]{0:T(128)}, u32[]{:S(2)}) copy-start(s32[2]{0:T(128)} %constant.153) | copy-start | bytes 28
  8.0 5.4 %copy-start.18 = (s32[2]{0:T(128)S(1)}, s32[2]{0:T(128)}, u32[]{:S(2)}) copy-start(s32[2]{0:T(128)} %constant.156) | copy-start | bytes 28
  46.9 6.4 %copy-start.22 = (s32[4]{0:T(128)S(1)}, s32[4]{0:T(128)}, u32[]{:S(2)}) copy-start(s32[4]{0:T(128)} %param.24) | copy-start | bytes 52
  46.9 7.0 %copy-start.4 = (s32[1280]{0:T(1024)S(1)}, s32[1280]{0:T(1024)}, u32[]{:S(2)}) copy-start(s32[1280]{0:T(1024)} %param.22) | copy-start | bytes 15364
  46.9 7.1 %copy-start.2 = (f32[31,320]{1,0:T(8,128)S(1)}, f32[31,320]{1,0:T(8,128)}, u32[]{:S(2)}) copy-start(f32[31,320]{1,0:T(8,128)} %param.19) | copy-start | bytes 119044
  46.9 38.9 %all-to-all-start = ((bf16[4,256,2,320]{1,3,2,0:T(8,128)(2,1)}), bf16[4,256,2,320]{1,3,2,0:T(8,128)(2,1)}, u32[]{:S(2)}, u32[]{:S(2)}) async-start(bf16[4,256,2,320]{1,3,2,0:T(8,128)(2,1)} %copy.23), calls=%async_computation | async-start | bytes 2621440 | tf_op jit(solution)/shard_map/all_to_all | solution.py:101
  62.2 4.0 %copy-start.21 = (f32[1280]{0:T(1024)S(1)}, f32[1280]{0:T(1024)}, u32[]{:S(2)}) copy-start(f32[1280]{0:T(1024)} %param.16) | copy-start | bytes 15364
  67.8 0.9 copy-start.1
  69.5 35.4 %collective-permute-start.1 = (bf16[320,2,320]{0,2,1:T(8,128)(2,1)}, bf16[320,2,320]{0,2,1:T(8,128)(2,1)}, u32[]{:S(2)}, u32[]{:S(2)}) collective-permute-start(bf16[320,2,320]{0,2,1:T(8,128)(2,1)} %slice.292), channel_id=1, source_target_pairs={{4,0},{8,4},{12,8},{5,1},{9,5},{13,9},{6,2},{10,6},{14,10},{7,3},{... | collective-permute-start | bytes 1228808 | tf_op jit(solution)/shard_map/ppermute | solution.py:20
  70.8 34.2 %collective-permute-start = (bf16[320,2,320]{0,2,1:T(8,128)(2,1)}, bf16[320,2,320]{0,2,1:T(8,128)(2,1)}, u32[]{:S(2)}, u32[]{:S(2)}) collective-permute-start(bf16[320,2,320]{0,2,1:T(8,128)(2,1)} %slice.292), channel_id=1, source_target_pairs={{0,4},{4,8},{8,12},{1,5},{5,9},{9,13},{2,6},{6,10},{10,14},{3,7},{... | collective-permute-start | bytes 1228808 | tf_op jit(solution)/shard_map/ppermute | solution.py:18
  106.7 1.2 slice-start
  118.0 15.4 %copy-start.20 = (bf16[1280,320]{0,1:T(8,128)(2,1)S(1)}, bf16[1280,320]{0,1:T(8,128)(2,1)}, u32[]{:S(2)}) copy-start(bf16[1280,320]{0,1:T(8,128)(2,1)} %param.18) | copy-start | bytes 2457604
  133.3 7.8 %copy-start.5 = (f32[320]{0:T(512)S(1)}, f32[320]{0:T(512)}, u32[]{:S(2)}) copy-start(f32[320]{0:T(512)} %get-tuple-element.13) | copy-start | bytes 3844
  133.3 7.8 %copy-start.6 = (f32[320]{0:T(512)S(1)}, f32[320]{0:T(512)}, u32[]{:S(2)}) copy-start(f32[320]{0:T(512)} %get-tuple-element.14) | copy-start | bytes 3844
  133.3 7.8 %copy-start.7 = (f32[320]{0:T(512)S(1)}, f32[320]{0:T(512)}, u32[]{:S(2)}) copy-start(f32[320]{0:T(512)} %get-tuple-element.15) | copy-start | bytes 3844
  133.3 7.8 %copy-start.8 = (f32[320]{0:T(512)S(1)}, f32[320]{0:T(512)}, u32[]{:S(2)}) copy-start(f32[320]{0:T(512)} %get-tuple-element.16) | copy-start | bytes 3844
  133.3 7.8 %copy-start.9 = (f32[320]{0:T(512)S(1)}, f32[320]{0:T(512)}, u32[]{:S(2)}) copy-start(f32[320]{0:T(512)} %get-tuple-element.17) | copy-start | bytes 3844
  133.4 7.8 %copy-start.10 = (f32[320]{0:T(512)S(1)}, f32[320]{0:T(512)}, u32[]{:S(2)}) copy-start(f32[320]{0:T(512)} %get-tuple-element.18) | copy-start | bytes 3844
  133.4 7.8 %copy-start.11 = (f32[320]{0:T(512)S(1)}, f32[320]{0:T(512)}, u32[]{:S(2)}) copy-start(f32[320]{0:T(512)} %get-tuple-element.19) | copy-start | bytes 3844
  133.4 7.8 %copy-start.12 = (f32[320]{0:T(512)S(1)}, f32[320]{0:T(512)}, u32[]{:S(2)}) copy-start(f32[320]{0:T(512)} %get-tuple-element.20) | copy-start | bytes 3844
  133.4 7.8 %copy-start.13 = (f32[320]{0:T(512)S(1)}, f32[320]{0:T(512)}, u32[]{:S(2)}) copy-start(f32[320]{0:T(512)} %get-tuple-element.21) | copy-start | bytes 3844
  133.4 7.8 %copy-start.14 = (f32[320]{0:T(512)S(1)}, f32[320]{0:T(512)}, u32[]{:S(2)}) copy-start(f32[320]{0:T(512)} %get-tuple-element.22) | copy-start | bytes 3844
  133.4 7.8 %copy-start.15 = (f32[320]{0:T(512)S(1)}, f32[320]{0:T(512)}, u32[]{:S(2)}) copy-start(f32[320]{0:T(512)} %get-tuple-element.23) | copy-start | bytes 3844
  133.4 7.8 %copy-start.16 = (f32[320]{0:T(512)S(1)}, f32[320]{0:T(512)}, u32[]{:S(2)}) copy-start(f32[320]{0:T(512)} %param.21) | copy-start | bytes 3844
  133.4 7.8 %copy-start.17 = (f32[320]{0:T(512)S(1)}, f32[320]{0:T(512)}, u32[]{:S(2)}) copy-start(f32[320]{0:T(512)} %param.20) | copy-start | bytes 3844
  134.2 3.7 %collective-permute-start.2 = (bf16[15,320]{1,0:T(8,128)(2,1)S(1)}, bf16[15,320]{1,0:T(8,128)(2,1)S(1)}, u32[]{:S(2)}, u32[]{:S(2)}) collective-permute-start(bf16[15,320]{1,0:T(8,128)(2,1)S(1)} %get-tuple-element.44), channel_id=1, source_target_pairs={{0,4},{4,8},{8,12},{1,5},{5,9},{9,13},{2,6},{6,10},{10,14},{3,7},{... | collective-permute-start | bytes 28808 | tf_op jit(solution)/shard_map/ppermute | solution.py:18
  135.5 5.6 %collective-permute-start.3 = (bf16[15,320]{1,0:T(8,128)(2,1)S(1)}, bf16[15,320]{1,0:T(8,128)(2,1)S(1)}, u32[]{:S(2)}, u32[]{:S(2)}) collective-permute-start(bf16[15,320]{1,0:T(8,128)(2,1)S(1)} %get-tuple-element.45), channel_id=1, source_target_pairs={{4,0},{8,4},{12,8},{5,1},{9,5},{13,9},{6,2},{10,6},{14,10},{7,3},{... | collective-permute-start | bytes 28808 | tf_op jit(solution)/shard_map/ppermute | solution.py:20
Sparse Core Ops, SparseCore 0:
  11.6 50.5 all-gather.2
